TPU v7x, 32 devices: a whole 2x2x4 slice. The times are simulated.
32 devices in a mesh: grp: 4 (over y, x), dev: 8 (over z, core).
Axes of the slice: x: 2, y: 2, z: 4, core: 2. Of those that a mesh axis runs over, the one named last changes fastest.
Arguments:
- amplitudes: float32 [2, 4, 8, 8192], P(None, 'grp', 'dev'), may hold values from -6 to 6
- joined_gates: float32 [4, 2, 128, 128], replicated, may hold values from -0.375 to 0.375
- pair_gate: float32 [2, 4, 4], replicated, may hold values from -2 to 2
- layout_in: int32 [18], replicated, may hold values from 0 to 17, as said below
- layout_out: int32 [18], replicated, may hold values from 0 to 17, as said below
- gate_qubits: int32 [4, 7], replicated, may hold values from 0 to 17, as said below
- spare_values: int32 [10], replicated, may hold values from 0 to 1
Outputs:
- evolved: float32 [2, 4, 8, 8192], P(None, 'grp', 'dev')
Inputs may be any that keep to these rules, and one draw needn't show every extreme that they name: `layout_in`: a permutation of the qubits. `layout_out`: a permutation of the qubits; entries 13 + 3 onward equal those of layout_in; entries 13 to 15 are qubits that layout_in holds below position 13. `gate_qubits`: each row holds 7 different qubits; rows 0 and 1 name qubits that layout_in holds below position 13, rows 2 and 3 qubits that layout_out holds below position 13.
All inputs are finite; a program needn't handle non-finite values.
Results may differ from a plain program's by a relative error of at most 0.0001.
Values sent between devices are 32-bit elements; how exact they have to be, the bound alone decides.
A program may use at most 64 MiB of HBM per device.

v0:
```python
import jax
import jax.numpy as jnp
from jax import lax
from jax.sharding import PartitionSpec as P

HIGHEST = lax.Precision.HIGHEST


def swapped(value, axis, bit):
    mask = 2**bit
    pairs = [(source, source ^ mask) for source in range(lax.axis_size(axis))]
    return lax.ppermute(value, axis, pairs)


def source_index(bit_order, bit_count):
    position = jnp.arange(2**bit_count, dtype=jnp.int32)
    source = jnp.zeros((2**bit_count,), jnp.int32)
    for place_bit in range(bit_count):
        source = source + jnp.left_shift(
            jnp.right_shift(position, place_bit) & 1, bit_order[place_bit]
        )
    return source


def reorder(values, source):
    return jnp.take(values, source_index(source, source.shape[0]), axis=1)


def complex_gate(values, matrix):
    real_part = jnp.dot(
        values[0], matrix[0].T, precision=HIGHEST, preferred_element_type=jnp.float32
    ) - jnp.dot(values[1], matrix[1].T, precision=HIGHEST, preferred_element_type=jnp.float32)
    imag_part = jnp.dot(
        values[0], matrix[1].T, precision=HIGHEST, preferred_element_type=jnp.float32
    ) + jnp.dot(values[1], matrix[0].T, precision=HIGHEST, preferred_element_type=jnp.float32)
    return jnp.stack([real_part, imag_part])


def pair_apply(values, pos_a, pos_c, matrix):
    count_all = values.shape[1]
    lower_pos = min(pos_a, pos_c)
    upper_pos = max(pos_a, pos_c)
    shaped = values.reshape(
        2, count_all >> upper_pos + 1, 2, 1 << upper_pos - lower_pos - 1, 2, 1 << lower_pos
    )
    tensor = matrix.reshape(2, 2, 2, 2, 2)
    pattern = "uvwx,hwmxl->humvl"
    real_part = jnp.einsum(pattern, tensor[0], shaped[0], precision=HIGHEST) - jnp.einsum(
        pattern, tensor[1], shaped[1], precision=HIGHEST
    )
    imag_part = jnp.einsum(pattern, tensor[1], shaped[0], precision=HIGHEST) + jnp.einsum(
        pattern, tensor[0], shaped[1], precision=HIGHEST
    )
    return jnp.stack([real_part, imag_part]).reshape(2, count_all)


def spare_sign(count_all, spare_values):
    position = jnp.arange(count_all, dtype=jnp.int32)
    parity = jnp.zeros((count_all,), jnp.int32)
    for place_bit in range(spare_values.shape[0]):
        parity = parity + spare_values[place_bit] * (jnp.right_shift(position, place_bit) & 1)
    return (1 - 2 * (parity & 1)).astype(jnp.float32)


def position_of(layout, wanted):
    places = jnp.arange(layout.shape[0], dtype=jnp.int32)
    return jnp.sum(jnp.where(layout[None, :] == wanted[:, None], places[None, :], 0), axis=1)


def arrange(layout, leading, trailing):
    layout_len = layout.shape[0]
    lead_count = leading.shape[0]
    trail_count = trailing.shape[0]
    in_lead = layout[:, None] == leading[None, :]
    in_trail = layout[:, None] == trailing[None, :]
    lead_any = jnp.any(in_lead, axis=1)
    trail_any = jnp.any(in_trail, axis=1)
    remaining = jnp.logical_not(jnp.logical_or(lead_any, trail_any)).astype(jnp.int32)
    lead_rank = jnp.sum(in_lead * jnp.arange(lead_count, dtype=jnp.int32)[None, :], axis=1)
    trail_rank = (
        layout_len
        - trail_count
        + jnp.sum(in_trail * jnp.arange(trail_count, dtype=jnp.int32)[None, :], axis=1)
    )
    target = jnp.where(
        lead_any,
        lead_rank,
        jnp.where(trail_any, trail_rank, lead_count + jnp.cumsum(remaining) - 1),
    )
    places = jnp.arange(layout_len, dtype=jnp.int32)
    source = jnp.zeros((layout_len,), jnp.int32).at[target].set(places)
    new_layout = jnp.zeros((layout_len,), jnp.int32).at[target].set(layout)
    return (new_layout, source)


def halves(values, place_bit):
    count_all = values.shape[1]
    shaped = values.reshape(2, count_all >> place_bit + 1, 2, 1 << place_bit)
    return (shaped[:, :, 0], shaped[:, :, 1])


def rejoin(lower_half, upper_half, received, own_bit):
    keep_lower = own_bit == 0
    new_lower = jnp.where(keep_lower, lower_half, received)
    new_upper = jnp.where(keep_lower, received, upper_half)
    return jnp.stack([new_lower, new_upper], axis=2).reshape(2, -1)


def trade_group(values, place_bit, bit_num):
    lower_half, upper_half = halves(values, place_bit)
    own_bit = jnp.right_shift(lax.axis_index("grp"), bit_num) & 1
    outgoing = jnp.where(own_bit == 0, upper_half, lower_half)
    received = swapped(outgoing, "grp", bit_num)
    return rejoin(lower_half, upper_half, received, own_bit)


def per_device(
    amplitudes, joined_gates, pair_gate, layout_in, layout_out, gate_qubits, spare_values
):
    length = amplitudes.shape[-1]
    local_bits = length.bit_length() - 1
    devices = lax.axis_size("dev")
    device_bits = devices.bit_length() - 1
    groups = lax.axis_size("grp")
    group_bits = groups.bit_length() - 1
    span_size = joined_gates.shape[-1]
    values = amplitudes.reshape(2, length)
    nothing = jnp.zeros((0,), jnp.int32)
    layout = layout_in[:local_bits]
    for gate_num in range(2):
        layout, source = arrange(layout, gate_qubits[gate_num], nothing)
        values = complex_gate(
            reorder(values, source).reshape(2, -1, span_size), joined_gates[gate_num]
        ).reshape(2, length)
    leaving = layout_out[local_bits : local_bits + device_bits]
    layout, source = arrange(layout, nothing, leaving)
    values = reorder(values, source)
    shaped = values.reshape(2, devices, length // devices)
    values = lax.all_to_all(shaped, "dev", split_axis=1, concat_axis=1, tiled=True).reshape(
        2, length
    )
    layout = jnp.concatenate(
        [layout[: local_bits - device_bits], layout_in[local_bits : local_bits + device_bits]]
    )
    for gate_num in range(2, 4):
        layout, source = arrange(layout, gate_qubits[gate_num], nothing)
        values = complex_gate(
            reorder(values, source).reshape(2, -1, span_size), joined_gates[gate_num]
        ).reshape(2, length)
    values = reorder(values, position_of(layout, layout_out[:local_bits]))
    values = values * spare_sign(length, spare_values)
    for bit_num in range(group_bits):
        place_bit = local_bits - 2 * group_bits + bit_num
        values = trade_group(values, place_bit, bit_num)
        values = pair_apply(values, place_bit, local_bits - 1 - bit_num, pair_gate)
        values = trade_group(values, place_bit, bit_num)
    return values.reshape(amplitudes.shape)


def solution(mesh):
    in_specs = (P(None, "grp", "dev", None), P(), P(), P(), P(), P(), P())
    out_specs = P(None, "grp", "dev", None)
    return jax.shard_map(
        per_device, mesh=mesh, in_specs=in_specs, out_specs=out_specs, check_vma=False
    )
```

profile of v0, /device:TPU:0, one launch (start us, length us, event | category | flops | bytes accessed | tf_op | source)
XLA Modules:
  0.0 406.6 jit_solution(7550245168328844921)
XLA Ops:
  0.0 0.8 slice_bitcast_fusion.2
  3.8 8.2 %broadcast_clamp_fusion.5 = s32[8192]{0:T(1024)S(1)} fusion(s32[]{:T(128)} %bitcast.96, s32[]{:T(128)} %bitcast.95, s32[]{:T(128)} %bitcast.94, s32[]{:T(128)} %bitcast.93, s32[]{:T(128)} %bitcast.92, s32[]{:T(128)} %bitcast.91, s32[]{:T(128)} %bitcast.90, s32[]{:T(128)} %bitcast.89, s32[]{:T(128)} %bitcast.88, s32[]{:T(128)} %bitcast.87, s32[]{:T(128)} %bitcast.86, ...), kind=kLoop, calls=%fused_computation.183 | loop fusion | flops 450560 | bytes 32820 | tf_op gather
  12.0 8.2 %compare_and_fusion.5 = pred[8192]{0:T(1024)(128)(4,1)S(1)} fusion(s32[]{:T(128)} %bitcast.96, s32[]{:T(128)} %bitcast.95, s32[]{:T(128)} %bitcast.94, s32[]{:T(128)} %bitcast.93, s32[]{:T(128)} %bitcast.92, s32[]{:T(128)} %bitcast.91, s32[]{:T(128)} %bitcast.90, s32[]{:T(128)} %bitcast.89, s32[]{:T(128)} %bitcast.88, s32[]{:T(128)} %bitcast.87, ...), kind=kLoop, calls=%fused_computation.172 | loop fusion | flops 466944 | bytes 8244 | tf_op jit(solution)/shard_map/jit(_take)/and | solution.py:26
  20.2 3.3 copy.134
  23.6 29.9 %gather_fusion = f32[8192,2]{1,0:T(8,128)} fusion(f32[2,8192]{0,1:T(8,128)} %bitcast.443, s32[8192]{0:T(1024)S(1)} %broadcast_clamp_fusion.5), kind=kCustom, calls=%fused_computation.clone | custom fusion | bytes 163840 | tf_op jit(solution)/shard_map/jit(_take)/gather | solution.py:26
  53.5 6.2 %select_bitcast_fusion.3 = f32[2,8192]{0,1:T(8,128)S(1)} fusion(f32[8192,2]{1,0:T(8,128)} %gather_fusion, pred[8192]{0:T(1024)(128)(4,1)S(1)} %compare_and_fusion.5), kind=kLoop, calls=%fused_computation.28 | loop fusion | flops 16384 | bytes 139264 | tf_op jit(solution)/shard_map/jit(_take)/select_n | solution.py:26
  59.7 3.3 slice_reduce_fusion.6
  65.9 8.2 %broadcast_clamp_fusion.4 = s32[8192]{0:T(1024)S(1)} fusion(s32[]{:T(128)} %bitcast.83, s32[]{:T(128)} %bitcast.82, s32[]{:T(128)} %bitcast.81, s32[]{:T(128)} %bitcast.80, s32[]{:T(128)} %bitcast.79, s32[]{:T(128)} %bitcast.78, s32[]{:T(128)} %bitcast.77, s32[]{:T(128)} %bitcast.76, s32[]{:T(128)} %bitcast.75, s32[]{:T(128)} %bitcast.74, s32[]{:T(128)} %bitcast.73, ...), kind=kLoop, calls=%fused_computation.182 | loop fusion | flops 450560 | bytes 32820 | tf_op gather
  74.1 8.2 %compare_and_fusion.4 = pred[8192]{0:T(1024)(128)(4,1)S(1)} fusion(s32[]{:T(128)} %bitcast.83, s32[]{:T(128)} %bitcast.82, s32[]{:T(128)} %bitcast.81, s32[]{:T(128)} %bitcast.80, s32[]{:T(128)} %bitcast.79, s32[]{:T(128)} %bitcast.78, s32[]{:T(128)} %bitcast.77, s32[]{:T(128)} %bitcast.76, s32[]{:T(128)} %bitcast.75, s32[]{:T(128)} %bitcast.74, ...), kind=kLoop, calls=%fused_computation.171 | loop fusion | flops 466944 | bytes 8244 | tf_op jit(solution)/shard_map/jit(_take)/and | solution.py:26
  82.9 2.6 copy.135
  85.5 29.9 %gather_fusion.1 = f32[8192,2]{1,0:T(8,128)} fusion(f32[2,8192]{0,1:T(8,128)} %copy.135, s32[8192]{0:T(1024)S(1)} %broadcast_clamp_fusion.4), kind=kCustom, calls=%fused_computation.1.clone | custom fusion | bytes 163840 | tf_op jit(solution)/shard_map/jit(_take)/gather | solution.py:26
  115.4 6.2 %select_bitcast_fusion.2 = f32[2,8192]{0,1:T(8,128)S(1)} fusion(f32[8192,2]{1,0:T(8,128)} %gather_fusion.1, pred[8192]{0:T(1024)(128)(4,1)S(1)} %compare_and_fusion.4), kind=kLoop, calls=%fused_computation.27 | loop fusion | flops 16384 | bytes 139264 | tf_op jit(solution)/shard_map/jit(_take)/select_n | solution.py:26
  121.7 3.3 slice_reduce_fusion.4
  128.1 8.2 %broadcast_clamp_fusion.3 = s32[8192]{0:T(1024)S(1)} fusion(s32[]{:T(128)} %bitcast.70, s32[]{:T(128)} %bitcast.69, s32[]{:T(128)} %bitcast.68, s32[]{:T(128)} %bitcast.67, s32[]{:T(128)} %bitcast.66, s32[]{:T(128)} %bitcast.65, s32[]{:T(128)} %bitcast.64, s32[]{:T(128)} %bitcast.63, s32[]{:T(128)} %bitcast.62, s32[]{:T(128)} %bitcast.61, s32[]{:T(128)} %bitcast.60, ...), kind=kLoop, calls=%fused_computation.181 | loop fusion | flops 450560 | bytes 32820 | tf_op gather
  136.3 8.2 %compare_and_fusion.3 = pred[8192]{0:T(1024)(128)(4,1)S(1)} fusion(s32[]{:T(128)} %bitcast.70, s32[]{:T(128)} %bitcast.69, s32[]{:T(128)} %bitcast.68, s32[]{:T(128)} %bitcast.67, s32[]{:T(128)} %bitcast.66, s32[]{:T(128)} %bitcast.65, s32[]{:T(128)} %bitcast.64, s32[]{:T(128)} %bitcast.63, s32[]{:T(128)} %bitcast.62, s32[]{:T(128)} %bitcast.61, ...), kind=kLoop, calls=%fused_computation.170 | loop fusion | flops 466944 | bytes 8244 | tf_op jit(solution)/shard_map/jit(_take)/and | solution.py:26
  145.0 2.6 copy.136
  147.7 29.9 %gather_fusion.2 = f32[8192,2]{1,0:T(8,128)} fusion(f32[2,8192]{0,1:T(8,128)} %copy.136, s32[8192]{0:T(1024)S(1)} %broadcast_clamp_fusion.3), kind=kCustom, calls=%fused_computation.2.clone | custom fusion | bytes 163840 | tf_op jit(solution)/shard_map/jit(_take)/gather | solution.py:26
  177.6 7.5 %broadcast_select_fusion = f32[8192,2]{1,0:T(8,128)} fusion(f32[8192,2]{1,0:T(8,128)} %gather_fusion.2, pred[8192]{0:T(1024)(128)(4,1)S(1)} %compare_and_fusion.3), kind=kLoop, calls=%fused_computation.29 | loop fusion | flops 16384 | bytes 139264 | tf_op jit(solution)/shard_map/jit(_take)/select_n | solution.py:26
  185.0 3.5 copy.137
  188.5 6.3 %all-to-all-start = ((f32[2,8,1024]{2,0,1:T(2,128)}), f32[2,8,1024]{2,0,1:T(2,128)S(1)}, u32[]{:S(2)}, u32[]{:S(2)}) async-start(f32[2,8,1024]{2,0,1:T(2,128)} %copy.137), calls=%async_computation | async-start | bytes 131072 | tf_op jit(solution)/shard_map/all_to_all | solution.py:139
  197.3 8.2 %broadcast_clamp_fusion.2 = s32[8192]{0:T(1024)S(1)} fusion(s32[]{:T(128)} %bitcast.57, s32[]{:T(128)} %bitcast.56, s32[]{:T(128)} %bitcast.55, s32[]{:T(128)} %bitcast.54, s32[]{:T(128)} %bitcast.53, s32[]{:T(128)} %bitcast.52, s32[]{:T(128)} %bitcast.51, s32[]{:T(128)} %bitcast.50, s32[]{:T(128)} %bitcast.49, s32[]{:T(128)} %bitcast.48, s32[]{:T(128)} %bitcast.47, ...), kind=kLoop, calls=%fused_computation.180 | loop fusion | flops 450560 | bytes 32820 | tf_op gather
  205.4 8.2 %compare_and_fusion.2 = pred[8192]{0:T(1024)(128)(4,1)S(1)} fusion(s32[]{:T(128)} %bitcast.57, s32[]{:T(128)} %bitcast.56, s32[]{:T(128)} %bitcast.55, s32[]{:T(128)} %bitcast.54, s32[]{:T(128)} %bitcast.53, s32[]{:T(128)} %bitcast.52, s32[]{:T(128)} %bitcast.51, s32[]{:T(128)} %bitcast.50, s32[]{:T(128)} %bitcast.49, s32[]{:T(128)} %bitcast.48, ...), kind=kLoop, calls=%fused_computation.169 | loop fusion | flops 466944 | bytes 8244 | tf_op jit(solution)/shard_map/jit(_take)/and | solution.py:26
  215.9 8.2 %broadcast_clamp_fusion.1 = s32[8192]{0:T(1024)S(1)} fusion(s32[]{:T(128)} %bitcast.44, s32[]{:T(128)} %bitcast.43, s32[]{:T(128)} %bitcast.42, s32[]{:T(128)} %bitcast.41, s32[]{:T(128)} %bitcast.40, s32[]{:T(128)} %bitcast.39, s32[]{:T(128)} %bitcast.38, s32[]{:T(128)} %bitcast.37, s32[]{:T(128)} %bitcast.36, s32[]{:T(128)} %bitcast.35, s32[]{:T(128)} %bitcast.34, ...), kind=kLoop, calls=%fused_computation.179 | loop fusion | flops 450560 | bytes 32820 | tf_op gather
  224.1 8.2 %compare_and_fusion.1 = pred[8192]{0:T(1024)(128)(4,1)S(1)} fusion(s32[]{:T(128)} %bitcast.44, s32[]{:T(128)} %bitcast.43, s32[]{:T(128)} %bitcast.42, s32[]{:T(128)} %bitcast.41, s32[]{:T(128)} %bitcast.40, s32[]{:T(128)} %bitcast.39, s32[]{:T(128)} %bitcast.38, s32[]{:T(128)} %bitcast.37, s32[]{:T(128)} %bitcast.36, s32[]{:T(128)} %bitcast.35, ...), kind=kLoop, calls=%fused_computation.168 | loop fusion | flops 466944 | bytes 8244 | tf_op jit(solution)/shard_map/jit(_take)/and | solution.py:26
  234.5 8.2 %broadcast_clamp_fusion = s32[8192]{0:T(1024)S(1)} fusion(s32[]{:T(128)} %bitcast.31, s32[]{:T(128)} %bitcast.30, s32[]{:T(128)} %bitcast.29, s32[]{:T(128)} %bitcast.28, s32[]{:T(128)} %bitcast.27, s32[]{:T(128)} %bitcast.26, s32[]{:T(128)} %bitcast.25, s32[]{:T(128)} %bitcast.24, s32[]{:T(128)} %bitcast.23, s32[]{:T(128)} %bitcast.22, s32[]{:T(128)} %bitcast.21, ...), kind=kLoop, calls=%fused_computation.178 | loop fusion | flops 450560 | bytes 32820 | tf_op gather
  242.6 8.2 %compare_and_fusion = pred[8192]{0:T(1024)(128)(4,1)S(1)} fusion(s32[]{:T(128)} %bitcast.31, s32[]{:T(128)} %bitcast.30, s32[]{:T(128)} %bitcast.29, s32[]{:T(128)} %bitcast.28, s32[]{:T(128)} %bitcast.27, s32[]{:T(128)} %bitcast.26, s32[]{:T(128)} %bitcast.25, s32[]{:T(128)} %bitcast.24, s32[]{:T(128)} %bitcast.23, s32[]{:T(128)} %bitcast.22, s32[]{:T(128)} %bitcast.21, ...), kind=kLoop, calls=%fused_computation.167 | loop fusion | flops 466944 | bytes 8244 | tf_op jit(solution)/shard_map/jit(_take)/and | solution.py:26
  250.8 6.2 %subtract_convert_fusion = f32[8192]{0:T(1024)S(1)} fusion(s32[]{:T(128)} %bitcast.131, s32[]{:T(128)} %bitcast.130, s32[]{:T(128)} %bitcast.129, s32[]{:T(128)} %bitcast.128, s32[]{:T(128)} %bitcast.127, s32[]{:T(128)} %bitcast.126, s32[]{:T(128)} %bitcast.125, s32[]{:T(128)} %bitcast.124, s32[]{:T(128)} %bitcast.123, s32[]{:T(128)} %bitcast.122), kind=kLoop, calls=%fused_computation.153 | loop fusion | flops 352256 | bytes 32808 | tf_op jit(solution)/shard_map/convert_element_type | solution.py:62
  257.1 2.6 copy.138
  259.7 29.9 %gather_fusion.3 = f32[8192,2]{1,0:T(8,128)} fusion(f32[2,8192]{0,1:T(8,128)} %bitcast.442, s32[8192]{0:T(1024)S(1)} %broadcast_clamp_fusion.2), kind=kCustom, calls=%fused_computation.3.clone | custom fusion | bytes 163840 | tf_op jit(solution)/shard_map/jit(_take)/gather | solution.py:26
  289.6 6.2 %select_bitcast_fusion.1 = f32[2,8192]{0,1:T(8,128)S(1)} fusion(f32[8192,2]{1,0:T(8,128)} %gather_fusion.3, pred[8192]{0:T(1024)(128)(4,1)S(1)} %compare_and_fusion.2), kind=kLoop, calls=%fused_computation.26 | loop fusion | flops 16384 | bytes 139264 | tf_op jit(solution)/shard_map/jit(_take)/select_n | solution.py:26
  295.8 3.3 slice_reduce_fusion.2
  300.2 2.6 copy.139
  302.8 29.9 %gather_fusion.4 = f32[8192,2]{1,0:T(8,128)} fusion(f32[2,8192]{0,1:T(8,128)} %copy.139, s32[8192]{0:T(1024)S(1)} %broadcast_clamp_fusion.1), kind=kCustom, calls=%fused_computation.4.clone | custom fusion | bytes 163840 | tf_op jit(solution)/shard_map/jit(_take)/gather | solution.py:26
  332.8 6.2 %select_bitcast_fusion = f32[2,8192]{0,1:T(8,128)S(1)} fusion(f32[8192,2]{1,0:T(8,128)} %gather_fusion.4, pred[8192]{0:T(1024)(128)(4,1)S(1)} %compare_and_fusion.1), kind=kLoop, calls=%fused_computation.25 | loop fusion | flops 16384 | bytes 139264 | tf_op jit(solution)/shard_map/jit(_take)/select_n | solution.py:26
  339.0 3.3 slice_reduce_fusion
  343.4 2.6 copy.140
  346.0 29.9 %gather_fusion.5 = f32[8192,2]{1,0:T(8,128)} fusion(f32[2,8192]{0,1:T(8,128)} %copy.140, s32[8192]{0:T(1024)S(1)} %broadcast_clamp_fusion), kind=kCustom, calls=%fused_computation.5.clone | custom fusion | bytes 163840 | tf_op jit(solution)/shard_map/jit(_take)/gather | solution.py:26
  375.9 6.2 %bitcast_multiply_fusion = f32[2,8192]{0,1:T(8,128)S(1)} fusion(f32[8192,2]{1,0:T(8,128)} %gather_fusion.5, f32[8192]{0:T(1024)S(1)} %subtract_convert_fusion, pred[8192]{0:T(1024)(128)(4,1)S(1)} %compare_and_fusion), kind=kLoop, calls=%fused_computation.24 | loop fusion | flops 32768 | bytes 172032 | tf_op jit(solution)/shard_map/mul | solution.py:151
  382.1 1.7 fusion.125
  383.8 2.2 copy.192
  386.7 1.6 collective-permute-start
  388.4 2.2 collective-permute-done
  392.1 1.6 collective-permute-start.1
  393.7 2.4 collective-permute-done.1
  396.4 1.6 collective-permute-start.2
  397.9 2.4 collective-permute-done.2
  401.8 1.6 collective-permute-start.3
  403.4 2.4 collective-permute-done.3
  (120 shorter events, 23.5 us)
Async XLA Ops:
  59.7 3.4 copy-start
  59.7 3.9 copy-start.3
  121.6 4.5 %copy-start.4 = (s32[18]{0:T(128)S(1)}, s32[18]{0:T(128)}, u32[]{:S(2)}) copy-start(s32[18]{0:T(128)} %param.13) | copy-start | bytes 220
  185.0 48.8 %copy-start.1 = (s32[10]{0:T(128)S(1)}, s32[10]{0:T(128)}, u32[]{:S(2)}) copy-start(s32[10]{0:T(128)} %param.15) | copy-start | bytes 124
  188.5 68.6 %all-to-all-start = ((f32[2,8,1024]{2,0,1:T(2,128)}), f32[2,8,1024]{2,0,1:T(2,128)S(1)}, u32[]{:S(2)}, u32[]{:S(2)}) async-start(f32[2,8,1024]{2,0,1:T(2,128)} %copy.137), calls=%async_computation | async-start | bytes 131072 | tf_op jit(solution)/shard_map/all_to_all | solution.py:139
  383.8 4.4 %copy-start.2 = (f32[2,4,4]{2,1,0:T(4,128)S(1)}, f32[2,4,4]{2,1,0:T(4,128)}, u32[]{:S(2)}) copy-start(f32[2,4,4]{2,1,0:T(4,128)} %param.11) | copy-start | bytes 388
  386.7 4.0 collective-permute-start
  392.1 4.0 collective-permute-start.1
  396.4 4.0 collective-permute-start.2
  401.8 4.0 collective-permute-start.3
where the time goes:
time: 409 us; the launch traced here: 407 us
  local copies, waits for them, and re-layouts  231 us (56%)
  other arithmetic  147 us (36%)
  starting transfers between devices  12.6 us (3%)
  waiting for transfers between devices  9.46 us (2%)
  matrix products  6.3 us (2%)
    gather x6, local copies, waits for them, and re-layouts, reorder(): return jnp.take(values, source_index(source, source.shape[0]), axis=1)  179 us
    and x6, other arithmetic, reorder(): return jnp.take(values, source_index(source, source.shape[0]), axis=1)  49.1 us
    gather x6, other arithmetic  49.1 us
    select_n x5, other arithmetic, reorder(): return jnp.take(values, source_index(source, source.shape[0]), axis=1)  32.3 us
    slice x4, local copies, waits for them, and re-layouts, complex_gate(): values[1]  13.3 us
    another operation x4, local copies, waits for them, and re-layouts, complex_gate(): return jnp.stack([real_part, imag_part])  10.5 us
    ppermute x4, waiting for transfers between devices, swapped(): return lax.ppermute(value, axis, pairs)  9.46 us
  transfers between devices with their start and end apart: 5, of which 4 were waited for; matrix products, arithmetic and copies ran while one was open for 15% of the time, Pallas kernels for 0%

commit v1 on v0

v1 whole, which is shorter than its diff:
```python
import functools

import jax
import jax.numpy as jnp
from jax import lax
from jax.experimental import pallas as pl
from jax.experimental.pallas import tpu as pltpu
from jax.sharding import PartitionSpec as P

MESH = pl.DeviceIdType.MESH
LANE_BITS = 7
SUB_BITS = 3


def bits_of(size):
    return size.bit_length() - 1


def split(x):
    high = x.astype(jnp.bfloat16)
    low = (x - high.astype(jnp.float32)).astype(jnp.bfloat16)
    return high, low


def nt_dot(a, b):
    return lax.dot_general(
        a, b, (((1,), (1,)), ((), ())), preferred_element_type=jnp.float32
    )


def nn_dot(a, b):
    return jnp.dot(a, b, preferred_element_type=jnp.float32)


def plan(in_lane, load):
    rows = len(in_lane) - LANE_BITS
    lane_shift, row_shift = [], []
    lanes_packed = rows_packed = shift = jnp.int32(0)
    for j in range(LANE_BITS):
        out = 1 - in_lane[j]
        lanes_packed = lanes_packed | jnp.left_shift(out * j, shift)
        lane_shift.append(shift)
        shift = shift + 4 * out
    shift = jnp.int32(0)
    for r in range(rows):
        moved = in_lane[LANE_BITS + r]
        rows_packed = rows_packed | jnp.left_shift(moved * r, shift)
        row_shift.append(shift)
        shift = shift + 4 * moved
    row_coef, row_layout = [], []
    for r in range(rows):
        moved = in_lane[LANE_BITS + r]
        partner = jnp.right_shift(lanes_packed, row_shift[r]) & 15
        row_coef.append(jnp.left_shift(moved, partner) & (2**LANE_BITS - 1))
        row_layout.append(load(jnp.where(moved == 1, jnp.minimum(partner, LANE_BITS - 1), LANE_BITS + r)))
    lane_coef, lane_layout = [], []
    for j in range(LANE_BITS):
        out = 1 - in_lane[j]
        partner = jnp.right_shift(rows_packed, lane_shift[j]) & 15
        lane_coef.append(jnp.left_shift(out, partner) & (2**rows - 1))
        lane_layout.append(load(jnp.where(out == 1, LANE_BITS + jnp.minimum(partner, rows - 1), j)))
    return row_coef, lane_coef, row_layout, lane_layout


def place_of(qubit, layout):
    found = jnp.int32(0)
    for p in range(1, len(layout)):
        found = found + jnp.where(layout[p] == qubit, p, 0)
    return found


def qubit_set(qubits):
    mask = jnp.int32(0)
    for q in qubits:
        mask = mask | jnp.left_shift(jnp.int32(1), q)
    return mask


def kernel(
    n_grp,
    n_dev,
    halves,
    amp_ref,
    gates_ref,
    pair_ref,
    lin_ref,
    lout_ref,
    gq_ref,
    spare_ref,
    out_ref,
    lay_ref,
    send_ref,
    recv_ref,
    gsend_ref,
    grecv_ref,
    dsend_sem,
    drecv_sem,
    gsend_sem,
    grecv_sem,
):
    grp, dev = lax.axis_index("grp"), lax.axis_index("dev")
    gb, db = bits_of(n_grp), bits_of(n_dev)
    n_rows = amp_ref.shape[1]
    row_bits = bits_of(n_rows)
    local = row_bits + LANE_BITS
    tiles = n_rows // 8
    tile_bits = row_bits - SUB_BITS

    barrier = pltpu.get_barrier_semaphore()
    for off in range(1, n_dev):
        pl.semaphore_signal(barrier, inc=1, device_id=(grp, dev ^ off), device_id_type=MESH)
    for k in range(gb):
        pl.semaphore_signal(
            barrier, inc=1, device_id=(grp ^ (1 << k), dev), device_id_type=MESH
        )

    lane = lax.broadcasted_iota(jnp.int32, (8, 128), 1)
    sub = lax.broadcasted_iota(jnp.int32, (8, 128), 0)
    lane_mask = [-(jnp.right_shift(lane, j) & 1) for j in range(LANE_BITS)]
    sub_mask = [-(jnp.right_shift(sub, j) & 1) for j in range(SUB_BITS)]

    def combine(masks, coefs):
        total = masks[0] & coefs[0]
        for m, c in zip(masks[1:], coefs[1:]):
            total = total ^ (m & c)
        return total

    def take(x, idx, axis):
        return jnp.take_along_axis(x, idx, axis=axis, mode="promise_in_bounds")

    def shear(x, row_coef, lane_coef, order):
        sub_part = combine(sub_mask, row_coef[:SUB_BITS])
        tile_part = []
        for v in range(tiles):
            part = jnp.int32(0)
            for i in range(tile_bits):
                if v >> i & 1:
                    part = part ^ row_coef[SUB_BITS + i]
            tile_part.append(part)
        first = lane ^ sub_part
        x = [[take(t[v], first ^ tile_part[v], 1) for v in range(tiles)] for t in x]
        rows = combine(lane_mask, lane_coef)
        for i in range(tile_bits):
            cond = (jnp.right_shift(rows, SUB_BITS + i) & 1) == 1
            x = [[jnp.where(cond, t[v ^ (1 << i)], t[v]) for v in range(tiles)] for t in x]
        subs = sub ^ (rows & 7)
        x = [[take(t[v], subs, 0) for v in range(tiles)] for t in x]
        last = sub_part ^ (lane if order is None else combine(lane_mask, order))
        return [[take(t[v], last ^ tile_part[v], 1) for v in range(tiles)] for t in x]

    def to_matrix(x):
        return jnp.concatenate(
            [jnp.concatenate(t, axis=0) for t in x], axis=1
        )

    def to_tiles(y):
        return [
            [y[8 * v : 8 * v + 8, 128 * c : 128 * c + 128] for v in range(tiles)]
            for c in range(2)
        ]

    def gate_plan(layout, slot, qubits):
        for p in range(local):
            lay_ref[slot, p] = layout[p]
        mask = qubit_set(qubits)
        in_lane = [jnp.right_shift(mask, layout[p]) & 1 for p in range(local)]
        rc, lc, row_layout, lane_layout = plan(in_lane, lambda i: lay_ref[slot, i])
        order = [
            jnp.left_shift(jnp.int32(1), place_of(q, lane_layout)) & (2**LANE_BITS - 1)
            for q in qubits
        ]
        return rc, lc, order, list(qubits) + row_layout

    def gate(x, g):
        u_re, u_im = gates_ref[g, 0], gates_ref[g, 1]
        w = jnp.concatenate(
            [
                jnp.concatenate([u_re, -u_im], axis=1),
                jnp.concatenate([u_im, u_re], axis=1),
            ],
            axis=0,
        )
        w_high, w_low = split(w)
        high, low = split(to_matrix(x))
        both = nt_dot(jnp.concatenate([high, low], axis=0), w_high)
        y = both[:n_rows] + (both[n_rows:] + nt_dot(high, w_low))
        return to_tiles(y)

    def row_permute(x, source):
        r_out = lax.broadcasted_iota(jnp.int32, (n_rows, n_rows), 0)
        r_in = lax.broadcasted_iota(jnp.int32, (n_rows, n_rows), 1)
        want = jnp.zeros_like(r_out)
        for i in range(row_bits):
            want = want | jnp.left_shift(jnp.right_shift(r_out, i) & 1, source[i])
        pick = jnp.where(want == r_in, 1.0, 0.0).astype(jnp.bfloat16)
        high, low = split(to_matrix(x))
        y = nn_dot(pick, jnp.concatenate([high, low], axis=1))
        return y[:, :256] + y[:, 256:]

    layout = [lin_ref[p] for p in range(local)]
    x = [[amp_ref[c, 8 * v : 8 * v + 8] for v in range(tiles)] for c in range(2)]
    for g in range(2):
        rc, lc, order, layout = gate_plan(layout, g, [gq_ref[g, i] for i in range(LANE_BITS)])
        x = gate(shear(x, rc, lc, order), g)

    leaving = [lout_ref[local + i] for i in range(db)]
    for p in range(local):
        lay_ref[2, p] = layout[p]
    mask = qubit_set(leaving)
    count = jnp.int32(0)
    in_lane = []
    for p in range(local):
        stays = 1 - (jnp.right_shift(mask, layout[p]) & 1)
        stays = jnp.where(count < LANE_BITS, stays, 0)
        in_lane.append(stays)
        count = count + stays
    rc, lc, row_layout, lane_layout = plan(in_lane, lambda i: lay_ref[2, i])
    packed = rank = jnp.int32(0)
    for r in range(row_bits):
        stays = 1 - (jnp.right_shift(mask, row_layout[r]) & 1)
        packed = packed | jnp.left_shift(stays * r, rank)
        rank = rank + 4 * stays
    for r in range(row_bits):
        lay_ref[3, r] = row_layout[r]
    source = [jnp.right_shift(packed, 4 * i) & 15 for i in range(row_bits - db)]
    stay_rows = [lay_ref[3, jnp.minimum(s, row_bits - 1)] for s in source]
    source = source + [place_of(q, row_layout) for q in leaving]
    y = row_permute(shear(x, rc, lc, None), source)
    layout = lane_layout + stay_rows + [lin_ref[local + i] for i in range(db)]

    depth = n_rows // n_dev
    for c in range(2):
        send_ref[:, c * depth : (c + 1) * depth, :] = y[:, 128 * c : 128 * c + 128].reshape(
            n_dev, depth, 128
        )
    recv_ref[dev] = send_ref[dev]

    pl.semaphore_wait(barrier, n_dev - 1 + gb)
    copies = []
    for off in range(n_dev - 1, 0, -1):
        copy = pltpu.make_async_remote_copy(
            src_ref=send_ref.at[dev ^ off],
            dst_ref=recv_ref.at[dev],
            send_sem=dsend_sem.at[off],
            recv_sem=drecv_sem.at[off],
            device_id=(grp, dev ^ off),
            device_id_type=MESH,
        )
        copy.start()
        copies.append(copy)

    rc, lc, order, layout = gate_plan(layout, 4, [gq_ref[2, i] for i in range(LANE_BITS)])
    for copy in copies:
        copy.wait_recv()
    x = []
    for c in range(2):
        flat = recv_ref[:, c * depth : (c + 1) * depth, :].reshape(n_rows, 128)
        x.append([flat[8 * v : 8 * v + 8] for v in range(tiles)])
    x = gate(shear(x, rc, lc, order), 2)
    rc, lc, order, layout = gate_plan(layout, 5, [gq_ref[3, i] for i in range(LANE_BITS)])
    x = gate(shear(x, rc, lc, order), 3)
    rc, lc, order, layout = gate_plan(layout, 6, [lout_ref[i] for i in range(LANE_BITS)])
    source = [place_of(lout_ref[LANE_BITS + i], layout[LANE_BITS:]) for i in range(row_bits)]
    y = row_permute(shear(x, rc, lc, order), source)

    spare = spare_ref.shape[0]
    flip = combine(lane_mask, [spare_ref[i] & 1 for i in range(min(spare, LANE_BITS))])
    position = lax.broadcasted_iota(jnp.int32, (n_rows, 128), 0)
    flip = jnp.concatenate([flip] * tiles, axis=0)
    for i in range(LANE_BITS, spare):
        flip = flip ^ (jnp.right_shift(position, i - LANE_BITS) & spare_ref[i] & 1)
    sign = (1 - 2 * (flip & 1)).astype(jnp.float32)
    x = to_tiles(y * jnp.concatenate([sign, sign], axis=1))

    def coefficient(c, row, col):
        return pair_ref[c, row, col]

    def pair_gate(own, other, k, names):
        a = jnp.right_shift(grp, k) & 1
        row_bit = row_bits - 1 - k
        if row_bit >= SUB_BITS:
            step = 1 << (row_bit - SUB_BITS)
            flipped = lambda t, v: t[v ^ step]
        else:
            step = 1 << row_bit
            flipped = lambda t, v: (
                jnp.where(
                    (sub & step) == 0, pltpu.roll(t[v], 8 - step, 0), pltpu.roll(t[v], step, 0)
                )
            )
        weights = {}
        for cbit in range(2):
            for src in range(2):
                for cs in range(2):
                    col = (a if src == 0 else 1 - a) + 2 * (cbit if cs == 0 else 1 - cbit)
                    weights[cbit, src, cs] = [
                        coefficient(part, a + 2 * cbit, col) for part in range(2)
                    ]
        out = [{}, {}]
        for v in names:
            re = im = None
            for src, data in enumerate((own, other)):
                for cs in range(2):
                    if row_bit >= SUB_BITS:
                        cbit = v >> (row_bit - SUB_BITS) & 1
                        w_re, w_im = weights[cbit, src, cs]
                    else:
                        high = (sub & step) != 0
                        w_re, w_im = [
                            jnp.where(high, weights[1, src, cs][p], weights[0, src, cs][p])
                            for p in range(2)
                        ]
                    d_re, d_im = [
                        data[c][v] if cs == 0 else flipped(data[c], v) for c in range(2)
                    ]
                    t_re = w_re * d_re - w_im * d_im
                    t_im = w_im * d_re + w_re * d_im
                    re = t_re if re is None else re + t_re
                    im = t_im if im is None else im + t_im
            out[0][v], out[1][v] = re, im
        return out

    groups = [[v for v in range(tiles) if v % halves == h] for h in range(halves)]
    held = [[{v: x[c][v] for v in names} for c in range(2)] for names in groups]
    count = tiles // halves
    pending = []
    for phase in range(gb):
        started = []
        for h, names in enumerate(groups):
            k = phase if h == 0 else gb - 1 - phase
            for c in range(2):
                for n, v in enumerate(names):
                    gsend_ref[phase, h, c, 8 * n : 8 * n + 8, :] = held[h][c][v]
            copy = pltpu.make_async_remote_copy(
                src_ref=gsend_ref.at[phase, h],
                dst_ref=grecv_ref.at[phase, h],
                send_sem=gsend_sem.at[phase, h],
                recv_sem=grecv_sem.at[phase, h],
                device_id=(grp ^ (1 << k), dev),
                device_id_type=MESH,
            )
            copy.start()
            started.append((h, names, k, copy))
        for h, names, k, copy in started:
            copy.wait_recv()
            other = [
                {v: grecv_ref[phase, h, c, 8 * n : 8 * n + 8, :] for n, v in enumerate(names)}
                for c in range(2)
            ]
            held[h] = pair_gate(held[h], other, k, names)
            pending.append(copy)
    for names, part in zip(groups, held):
        for c in range(2):
            for v in names:
                out_ref[c, 8 * v : 8 * v + 8, :] = part[c][v]
    for copy in copies + pending:
        copy.wait_send()


def per_device(
    amplitudes, joined_gates, pair_gate, layout_in, layout_out, gate_qubits, spare_values
):
    n_grp, n_dev = lax.axis_size("grp"), lax.axis_size("dev")
    gb = bits_of(n_grp)
    n_rows = amplitudes.shape[-1] // 128
    tiles = n_rows // 8
    halves = 2 if gb == 2 else 1
    values = amplitudes.reshape(2, n_rows, 128)
    vmem = pl.BlockSpec(memory_space=pltpu.VMEM)
    smem = pl.BlockSpec(memory_space=pltpu.SMEM)
    depth = n_rows // n_dev
    out = pl.pallas_call(
        functools.partial(kernel, n_grp, n_dev, halves),
        out_shape=jax.ShapeDtypeStruct(values.shape, jnp.float32),
        in_specs=[vmem, vmem, smem, smem, smem, smem, smem],
        out_specs=vmem,
        scratch_shapes=[
            pltpu.SMEM((8, 16), jnp.int32),
            pltpu.VMEM((n_dev, 2 * depth, 128), jnp.float32),
            pltpu.VMEM((n_dev, 2 * depth, 128), jnp.float32),
            pltpu.VMEM((gb, halves, 2, n_rows // halves, 128), jnp.float32),
            pltpu.VMEM((gb, halves, 2, n_rows // halves, 128), jnp.float32),
            pltpu.SemaphoreType.DMA((n_dev,)),
            pltpu.SemaphoreType.DMA((n_dev,)),
            pltpu.SemaphoreType.DMA((gb, halves)),
            pltpu.SemaphoreType.DMA((gb, halves)),
        ],
        compiler_params=pltpu.CompilerParams(
            collective_id=0, has_side_effects=True, vmem_limit_bytes=32 * 1024 * 1024
        ),
    )(values, joined_gates, pair_gate, layout_in, layout_out, gate_qubits, spare_values)
    return out.reshape(amplitudes.shape)


def solution(mesh):
    in_specs = (P(None, "grp", "dev", None), P(), P(), P(), P(), P(), P())
    out_specs = P(None, "grp", "dev", None)
    return jax.shard_map(
        per_device, mesh=mesh, in_specs=in_specs, out_specs=out_specs, check_vma=False
    )
```

time: 409 us -> 21.9 us (0.05)
  local copies, waits for them, and re-layouts: 231 us -> 4.56 us
  other arithmetic: 147 us -> 0 us
  Pallas kernels: 0 us -> 17 us
  starting transfers between devices: 12.6 us -> 0 us
  waiting for transfers between devices: 9.46 us -> 0 us
  matrix products: 6.3 us -> 0 us
    gather x6 -> x0, local copies, waits for them, and re-layouts: 179 us -> none  [reorder(): return jnp.take(values, source_index(source, source.shape[0]), axis=1)]
    and x6 -> x0, other arithmetic: 49.1 us -> none  [reorder(): return jnp.take(values, source_index(source, source.shape[0]), axis=1)]
    gather x6 -> x0, other arithmetic: 49.1 us -> none
    select_n x14 -> x0, other arithmetic: 32.4 us -> none  [the longest x5 32.3 us: reorder(): return jnp.take(values, source_index(source, source.shape[0]), axis=1)]
    slice x20 -> x0, local copies, waits for them, and re-layouts: 20.2 us -> none  [the longest x4 13.3 us: complex_gate(): values[1]]
    pallas_call x0 -> x1, Pallas kernels: none -> 17 us  [per_device(): pl.pallas_call(functools.partial(kernel, n_grp, n_dev, halves), out_shape...]
    another operation x9 -> x0, local copies, waits for them, and re-layouts: 11.4 us -> none  [the longest x4 10.5 us: complex_gate(): return jnp.stack([real_part, imag_part])]
    ppermute x4 -> x0, waiting for transfers between devices: 9.46 us -> none  [swapped(): return lax.ppermute(value, axis, pairs)]
  transfers between devices with their start and end apart: 5 -> 0, of which waited for: 4 -> 0; matrix products, arithmetic and copies ran while one was open for 15% -> 0% of each run, Pallas kernels for 0% -> 0%
where the time goes in v1:
time: 21.9 us; the launch traced here: 21.6 us
  Pallas kernels  17 us (78%)
  local copies, waits for them, and re-layouts  4.56 us (21%)
    pallas_call x1, Pallas kernels, per_device(): pl.pallas_call(functools.partial(kernel, n_grp, n_dev, halves), out_shape...  17 us
    unnamed x15, local copies, waits for them, and re-layouts  4.56 us

profile of v1, /device:TPU:0, one launch (start us, length us, event | category | flops | bytes accessed | tf_op | source)
XLA Modules:
  0.0 21.6 jit_solution(17426843209777554112)
XLA Ops:
  0.0 0.0 copy-start.6
  0.0 0.0 copy-start.5
  0.0 0.0 copy-start.4
  0.0 0.6 %copy-done.6 = s32[10]{0:T(128)S(1)} copy-done((s32[10]{0:T(128)S(1)}, s32[10]{0:T(128)}, u32[]{:S(2)}) %copy-start.6) | copy-done | bytes 64
  0.7 0.0 copy-done.5
  0.7 0.0 copy-done.4
  0.7 0.0 copy-start
  0.7 1.0 %copy-done = f32[4,2,128,128]{3,2,1,0:T(8,128)S(1)} copy-done((f32[4,2,128,128]{3,2,1,0:T(8,128)S(1)}, f32[4,2,128,128]{3,2,1,0:T(8,128)}, u32[]{:S(2)}) %copy-start) | copy-done | bytes 524312
  1.7 0.0 copy-start.1
  1.7 0.8 %copy-done.1 = f32[2,1,1,8192]{3,2,1,0:T(1,128)S(1)} copy-done((f32[2,1,1,8192]{3,2,1,0:T(1,128)S(1)}, f32[2,1,1,8192]{3,2,1,0:T(1,128)}, u32[]{:S(2)}) %copy-start.1) | copy-done | bytes 65560
  2.6 0.0 copy-start.2
  2.6 0.7 %copy-done.2 = f32[2,4,4]{2,1,0:T(4,128)S(1)} copy-done((f32[2,4,4]{2,1,0:T(4,128)S(1)}, f32[2,4,4]{2,1,0:T(4,128)}, u32[]{:S(2)}) %copy-start.2) | copy-done | bytes 152
  3.3 0.0 copy-start.3
  3.3 0.7 %copy-done.3 = s32[4,7]{1,0:T(4,128)S(1)} copy-done((s32[4,7]{1,0:T(4,128)S(1)}, s32[4,7]{1,0:T(4,128)}, u32[]{:S(2)}) %copy-start.3) | copy-done | bytes 136
  3.9 17.0 %shard_map.73 = f32[2,64,128]{2,1,0:T(8,128)S(1)} custom-call(f32[2,64,128]{2,1,0:T(8,128)S(1)} %bitcast.3, f32[4,2,128,128]{3,2,1,0:T(8,128)S(1)} %copy-done, f32[2,4,4]{2,1,0:T(4,128)S(1)} %copy-done.2, s32[18]{0:T(128)S(1)} %copy-done.4, s32[18]{0:T(128)S(1)} %copy-done.5, s32[4,7]{1,0:T(4,128)S(1)} %copy-done.3, s32[10]{0:T(128)S(1)} %copy-done.6), custom_call_target="tpu_custom_call" | custom-call | tf_op jit(solution)/shard_map/pallas_call | solution.py:372
  21.0 0.6 %copy.10 = f32[2,1,1,8192]{3,2,1,0:T(1,128)} copy(f32[2,1,1,8192]{3,2,1,0:T(1,128)S(1)} %bitcast.2) | data formatting | bytes 131072
Async XLA Ops:
  0.0 0.7 %copy-start.6 = (s32[10]{0:T(128)S(1)}, s32[10]{0:T(128)}, u32[]{:S(2)}) copy-start(s32[10]{0:T(128)} %spare_ref.1) | copy-start | bytes 124
  0.0 0.7 %copy-start.5 = (s32[18]{0:T(128)S(1)}, s32[18]{0:T(128)}, u32[]{:S(2)}) copy-start(s32[18]{0:T(128)} %lout_ref.1) | copy-start | bytes 220
  0.0 0.7 %copy-start.4 = (s32[18]{0:T(128)S(1)}, s32[18]{0:T(128)}, u32[]{:S(2)}) copy-start(s32[18]{0:T(128)} %lin_ref.1) | copy-start | bytes 220
  0.7 1.0 %copy-start = (f32[4,2,128,128]{3,2,1,0:T(8,128)S(1)}, f32[4,2,128,128]{3,2,1,0:T(8,128)}, u32[]{:S(2)}) copy-start(f32[4,2,128,128]{3,2,1,0:T(8,128)} %gates_ref.1) | copy-start | bytes 1572868
  1.7 0.8 %copy-start.1 = (f32[2,1,1,8192]{3,2,1,0:T(1,128)S(1)}, f32[2,1,1,8192]{3,2,1,0:T(1,128)}, u32[]{:S(2)}) copy-start(f32[2,1,1,8192]{3,2,1,0:T(1,128)} %param.7) | copy-start | bytes 196612
  2.6 0.7 %copy-start.2 = (f32[2,4,4]{2,1,0:T(4,128)S(1)}, f32[2,4,4]{2,1,0:T(4,128)}, u32[]{:S(2)}) copy-start(f32[2,4,4]{2,1,0:T(4,128)} %pair_ref.1) | copy-start | bytes 388
  3.3 0.7 %copy-start.3 = (s32[4,7]{1,0:T(4,128)S(1)}, s32[4,7]{1,0:T(4,128)}, u32[]{:S(2)}) copy-start(s32[4,7]{1,0:T(4,128)} %gq_ref.1) | copy-start | bytes 340

commit v2 on v1

--- a/solution.py
+++ b/solution.py
@@ -81,7 +81,7 @@
     n_dev,
     halves,
     amp_ref,
-    gates_ref,
+    gates_hbm,
     pair_ref,
     lin_ref,
     lout_ref,
@@ -97,7 +97,15 @@
     drecv_sem,
     gsend_sem,
     grecv_sem,
+    gates_ref,
+    gates_sem,
 ):
+    fetches = [
+        pltpu.make_async_copy(gates_hbm.at[g], gates_ref.at[g], gates_sem.at[g])
+        for g in range(4)
+    ]
+    for fetch in fetches:
+        fetch.start()
     grp, dev = lax.axis_index("grp"), lax.axis_index("dev")
     gb, db = bits_of(n_grp), bits_of(n_dev)
     n_rows = amp_ref.shape[1]
@@ -172,6 +180,7 @@
         return rc, lc, order, list(qubits) + row_layout
 
     def gate(x, g):
+        fetches[g].wait()
         u_re, u_im = gates_ref[g, 0], gates_ref[g, 1]
         w = jnp.concatenate(
             [
@@ -372,7 +381,7 @@
     out = pl.pallas_call(
         functools.partial(kernel, n_grp, n_dev, halves),
         out_shape=jax.ShapeDtypeStruct(values.shape, jnp.float32),
-        in_specs=[vmem, vmem, smem, smem, smem, smem, smem],
+        in_specs=[vmem, pl.BlockSpec(memory_space=pl.ANY), smem, smem, smem, smem, smem],
         out_specs=vmem,
         scratch_shapes=[
             pltpu.SMEM((8, 16), jnp.int32),
@@ -384,9 +393,11 @@
             pltpu.SemaphoreType.DMA((n_dev,)),
             pltpu.SemaphoreType.DMA((gb, halves)),
             pltpu.SemaphoreType.DMA((gb, halves)),
+            pltpu.VMEM(joined_gates.shape, jnp.float32),
+            pltpu.SemaphoreType.DMA((4,)),
         ],
         compiler_params=pltpu.CompilerParams(
-            collective_id=0, has_side_effects=True, vmem_limit_bytes=32 * 1024 * 1024
+            collective_id=0, has_side_effects=True, vmem_limit_bytes=60 * 1024 * 1024
         ),
     )(values, joined_gates, pair_gate, layout_in, layout_out, gate_qubits, spare_values)
     return out.reshape(amplitudes.shape)

time: 21.9 us -> 20.4 us (0.932)
  local copies, waits for them, and re-layouts: 4.56 us -> 1.47 us
  Pallas kernels: 17 us -> 18.7 us
    unnamed x15 -> x1, local copies, waits for them, and re-layouts: 4.56 us -> 1.47 us
    pallas_call x1, Pallas kernels: 17 us -> 18.7 us  [per_device(): pl.pallas_call(functools.partial(kernel, n_grp, n_dev, halves), out_shape...]
where the time goes in v2:
time: 20.4 us; the launch traced here: 20.2 us
  Pallas kernels  18.7 us (92%)
  local copies, waits for them, and re-layouts  1.47 us (7%)
    pallas_call x1, Pallas kernels, per_device(): pl.pallas_call(functools.partial(kernel, n_grp, n_dev, halves), out_shape...  18.7 us
    unnamed x1, local copies, waits for them, and re-layouts  1.47 us

profile of v2, /device:TPU:0, one launch (start us, length us, event | category | flops | bytes accessed | tf_op | source)
XLA Modules:
  0.0 20.2 jit_solution(11626607461773114174)
XLA Ops:
  0.0 18.7 %shard_map.73 = f32[2,64,128]{2,1,0:T(8,128)} custom-call(f32[2,64,128]{2,1,0:T(8,128)} %bitcast.3, f32[4,2,128,128]{3,2,1,0:T(8,128)} %gates_hbm.1, f32[2,4,4]{2,1,0:T(4,128)} %pair_ref.1, s32[18]{0:T(128)} %lin_ref.1, s32[18]{0:T(128)} %lout_ref.1, s32[4,7]{1,0:T(4,128)} %gq_ref.1, s32[10]{0:T(128)} %spare_ref.1), custom_call_target="tpu_custom_call" | custom-call | tf_op jit(solution)/shard_map/pallas_call | solution.py:381
  18.7 1.5 %copy.10 = f32[2,1,1,8192]{3,2,1,0:T(1,128)} copy(f32[2,1,1,8192]{3,2,1,0:T(1,128)} %bitcast.2) | data formatting | bytes 131072
